TPU v7x, 256 devices: a whole 4x4x8 slice. The times are simulated.
256 devices in a mesh: slab: 64 (over z, y, x_hi), quad: 4 (over x_lo, core).
Axes of the slice: x: 4 (x_hi: 2, x_lo: 2; x = x_hi * 2 + x_lo), y: 4, z: 8, core: 2. Of those that a mesh axis runs over, the one named last changes fastest.
Arguments:
- rhs: float32 [64, 4, 4, 192, 256], P('slab', 'quad'), may hold values from -6 to 6
- blocks: bfloat16 [64, 4, 4, 26, 192, 192], P('slab', 'quad'), may hold values from -0.03125 to 0.03125
- diag_blocks: bfloat16 [64, 4, 4, 192, 192], P('slab', 'quad'), may hold values from -0.2 to 1.2
- neighbours: int32 [64, 4, 4, 26], P('slab', 'quad'), may hold values from 0 to 25, each once within a row
- bound: float32 [1], replicated, may hold values from 1.9 to 2.6
- restrict_blocks: bfloat16 [8, 192, 192], replicated, may hold values from -0.21875 to 0.21875
- restrict_kind: int32 [64, 4, 4], P('slab', 'quad'), may hold values from 0 to 7
Outputs:
- smoothed: float32 [64, 4, 4, 192, 256], P('slab', 'quad')
- coarse: float32 [64, 4, 1, 192, 256], P('slab', 'quad')
Inputs may be any that keep to these rules, and one draw needn't show every extreme that they name: `neighbours`: each block row names each of its 26 neighbour offsets once.
All inputs are finite; a program needn't handle non-finite values.
Results may differ from a plain program's by a relative error of at most 0.0074.
Values may be sent and summed in bfloat16 or wider, within the bound.
A program may use at most 128 MiB of HBM per device.

v0:
```python
import jax
import jax.numpy as jnp
from jax import lax
from jax.sharding import PartitionSpec as P


def extended(cells, sides, width):
    for axis, dim in sides:
        count = lax.axis_size(axis)
        ends = count - 1
        head = lax.slice_in_dim(cells, 0, width, axis=dim)
        tail = lax.slice_in_dim(cells, cells.shape[dim] - width, cells.shape[dim], axis=dim)
        cells = jnp.concatenate(
            [
                lax.ppermute(tail, axis, [(i, (i + 1) % count) for i in range(ends)]),
                cells,
                lax.ppermute(head, axis, [((i + 1) % count, i) for i in range(ends)]),
            ],
            axis=dim,
        )
    return cells


def from_partner(value, axis, distance):
    mask = 2**distance
    pairs = [(source, source ^ mask) for source in range(lax.axis_size(axis))]
    return lax.ppermute(value, axis, pairs)


def offsets_of(neighbours):
    offset = neighbours + (neighbours >= 13).astype(jnp.int32)
    return (offset // 9, offset // 3 % 3, offset % 3)


def apply_local(vector_bf, diag_blocks, blocks, neighbours):
    padded = extended(vector_bf, (("slab", 0), ("quad", 1)), 1)
    padded = jnp.pad(padded, ((0, 0), (0, 0), (1, 1), (0, 0), (0, 0)))
    width = vector_bf.shape[2]
    flat = padded.reshape((9 * (width + 2),) + padded.shape[3:])
    depth_off, row_off, col_off = offsets_of(neighbours[0, 0])
    xpos = jnp.arange(width, dtype=jnp.int32)[:, None]
    flat_index = depth_off * (3 * (width + 2)) + row_off * (width + 2) + xpos + col_off
    gathered = flat[flat_index]
    image = jnp.einsum("xsij,xsjn->xin", blocks[0, 0], gathered, preferred_element_type=jnp.float32)
    image = image + jnp.einsum(
        "xij,xjn->xin", diag_blocks[0, 0], vector_bf[0, 0], preferred_element_type=jnp.float32
    )
    return image[None, None]


def on_device(rhs, blocks, diag_blocks, neighbours, bound, restrict_blocks, restrict_kind):
    theta = 9.0 * bound[0] / 16.0
    delta = 7.0 * bound[0] / 16.0
    sigma = 9.0 / 7.0
    rho_prev = 1.0 / sigma
    residual = rhs
    direction = residual / theta
    smoothed = direction
    for section in range(3):
        image = apply_local(direction.astype(jnp.bfloat16), diag_blocks, blocks, neighbours)
        residual = residual - image
        if section < 2:
            rho_next = 1.0 / (2.0 * sigma - rho_prev)
            direction = rho_next * rho_prev * direction + 2.0 * rho_next / delta * residual
            smoothed = smoothed + direction
            rho_prev = rho_next
    fine = residual.astype(jnp.bfloat16)
    chosen = restrict_blocks[restrict_kind[0, 0]]
    terms = jnp.einsum("xij,xjn->xin", chosen, fine[0, 0], preferred_element_type=jnp.float32)
    width = terms.shape[0]
    paired = terms.reshape((width // 4, 2, 2) + terms.shape[1:]).sum(axis=2)
    parity = lax.axis_index("slab") % 2
    keeper = jnp.where(parity == 0, paired[:, 0], paired[:, 1])
    sender = jnp.where(parity == 0, paired[:, 1], paired[:, 0])
    arrived = from_partner(sender.astype(jnp.bfloat16), "slab", 0).astype(sender.dtype)
    coarse = keeper + arrived
    return (smoothed, coarse[None, None])


def solution(mesh):
    return jax.shard_map(
        on_device,
        mesh=mesh,
        in_specs=(
            P("slab", "quad", None, None, None),
            P("slab", "quad", None, None, None, None),
            P("slab", "quad", None, None, None),
            P("slab", "quad", None, None),
            P(),
            P(),
            P("slab", "quad", None),
        ),
        out_specs=(P("slab", "quad", None, None, None), P("slab", "quad", None, None, None)),
        check_vma=False,
    )
```

profile of v0, /device:TPU:125, one launch (start us, length us, event | category | flops | bytes accessed | tf_op | source)
XLA Modules:
  0.0 208.7 jit_solution(17755520437378588459)
XLA Ops:
  0.6 0.0 copy-start
  1.4 1.2 fusion.49
  2.6 4.4 %collective-permute-start = (bf16[1,1,4,192,256]{4,3,2,1,0:T(8,128)(2,1)S(1)}, bf16[1,1,4,192,256]{4,3,2,1,0:T(8,128)(2,1)S(1)}, u32[]{:S(2)}, u32[]{:S(2)}) collective-permute-start(bf16[1,1,4,192,256]{4,3,2,1,0:T(8,128)(2,1)S(1)} %fusion.49), channel_id=1, source_target_pairs={{0,4},{4,8},{8,12},{12,16},{16,20},{20,24},{24,28},{28,32},{32,36}... | collective-permute-start | bytes 1179656 | tf_op jit(solution)/shard_map/ppermute | solution.py:15
  6.9 2.4 %collective-permute-start.1 = (bf16[1,1,4,192,256]{4,3,2,1,0:T(8,128)(2,1)S(1)}, bf16[1,1,4,192,256]{4,3,2,1,0:T(8,128)(2,1)S(1)}, u32[]{:S(2)}, u32[]{:S(2)}) collective-permute-start(bf16[1,1,4,192,256]{4,3,2,1,0:T(8,128)(2,1)S(1)} %fusion.49), channel_id=1, source_target_pairs={{4,0},{8,4},{12,8},{16,12},{20,16},{24,20},{28,24},{32,28},{36,32}... | collective-permute-start | bytes 1179656 | tf_op jit(solution)/shard_map/ppermute | solution.py:17
  9.4 6.6 %collective-permute-done = bf16[1,1,4,192,256]{4,3,2,1,0:T(8,128)(2,1)S(1)} collective-permute-done((bf16[1,1,4,192,256]{4,3,2,1,0:T(8,128)(2,1)S(1)}, bf16[1,1,4,192,256]{4,3,2,1,0:T(8,128)(2,1)S(1)}, u32[]{:S(2)}, u32[]{:S(2)}) %collective-permute-start) | collective-permute-done | bytes 393248 | tf_op jit(solution)/shard_map/ppermute | solution.py:15
  15.9 8.3 %collective-permute-done.1 = bf16[1,1,4,192,256]{4,3,2,1,0:T(8,128)(2,1)S(1)} collective-permute-done((bf16[1,1,4,192,256]{4,3,2,1,0:T(8,128)(2,1)S(1)}, bf16[1,1,4,192,256]{4,3,2,1,0:T(8,128)(2,1)S(1)}, u32[]{:S(2)}, u32[]{:S(2)}) %collective-permute-start.1) | collective-permute-done | bytes 393248 | tf_op jit(solution)/shard_map/ppermute | solution.py:17
  24.2 1.1 pad_maximum_fusion
  25.4 5.5 %collective-permute-start.2 = (bf16[3,1,4,192,256]{4,3,2,1,0:T(8,128)(2,1)}, bf16[3,1,4,192,256]{4,3,2,1,0:T(8,128)(2,1)S(1)}, u32[]{:S(2)}, u32[]{:S(2)}) collective-permute-start(bf16[3,1,4,192,256]{4,3,2,1,0:T(8,128)(2,1)} %pad_maximum_fusion), channel_id=1, source_target_pairs={{0,1},{1,2},{2,3},{4,5},{5,6},{6,7},{8,9},{9,10},{10,11},{12,13},{... | collective-permute-start | bytes 3538952 | tf_op jit(solution)/shard_map/ppermute | solution.py:15
  30.8 1.9 collective-permute-start.3
  32.8 0.7 compare_select_fusion
  33.5 0.1 reshape.233
  33.6 10.7 %collective-permute-done.2 = bf16[3,1,4,192,256]{4,3,2,1,0:T(8,128)(2,1)S(1)} collective-permute-done((bf16[3,1,4,192,256]{4,3,2,1,0:T(8,128)(2,1)}, bf16[3,1,4,192,256]{4,3,2,1,0:T(8,128)(2,1)S(1)}, u32[]{:S(2)}, u32[]{:S(2)}) %collective-permute-start.2) | collective-permute-done | bytes 1179680 | tf_op jit(solution)/shard_map/ppermute | solution.py:15
  44.3 4.4 %collective-permute-done.3 = bf16[3,1,4,192,256]{4,3,2,1,0:T(8,128)(2,1)} collective-permute-done((bf16[3,1,4,192,256]{4,3,2,1,0:T(8,128)(2,1)}, bf16[3,1,4,192,256]{4,3,2,1,0:T(8,128)(2,1)}, u32[]{:S(2)}, u32[]{:S(2)}) %collective-permute-start.3) | collective-permute-done | bytes 1179680 | tf_op jit(solution)/shard_map/ppermute | solution.py:17
  48.7 4.1 %select_maximum_fusion.8 = bf16[3,3,6,192,256]{4,3,2,1,0:T(8,128)(2,1)} fusion(bf16[3,1,4,192,256]{4,3,2,1,0:T(8,128)(2,1)} %collective-permute-done.3, bf16[3,1,4,192,256]{4,3,2,1,0:T(8,128)(2,1)S(1)} %collective-permute-done.2, bf16[1,1,4,192,256]{4,3,2,1,0:T(8,128)(2,1)S(1)} %collective-permute-done.1, bf16[1,1,4,192,256]{4,3,2,1,0:T(8,128)(2,1)S(1)} %fusion.49, ...), kind=kLoop, calls=%fused_computation.21 | loop fusion | flops 47775744 | bytes 8847360 | tf_op jit(solution)/shard_map/concatenate | solution.py:13
  52.8 10.3 %gather_fusion = bf16[104,192,256]{2,1,0:T(8,128)(2,1)} fusion(bf16[54,192,256]{2,1,0:T(8,128)(2,1)} %bitcast.117, s32[1024]{0:T(1024)S(1)} %pad_clamp_fusion.1), kind=kCustom, calls=%fused_computation | custom fusion | bytes 20447648 | tf_op jit(solution)/shard_map/gather | solution.py:43
  63.0 10.1 %fusion.21 = f32[4,256,192]{1,2,0:T(8,128)S(1)} fusion(bf16[4,26,192,256]{3,2,1,0:T(8,128)(2,1)} %bitcast.121, bf16[1,1,4,26,192,192]{5,4,3,2,1,0:T(8,128)(2,1)} %param.8), kind=kOutput, calls=%fused_computation.36 | convolution fusion | flops 1962934272 | bytes 18677760 | tf_op jit(solution)/shard_map/xsij,xsjn->xin/dot_general | solution.py:44
  73.2 0.3 fusion.40
  73.5 4.6 %collective-permute-start.4 = (bf16[1,1,4,192,256]{4,3,2,1,0:T(8,128)(2,1)S(1)}, bf16[1,1,4,192,256]{4,3,2,1,0:T(8,128)(2,1)S(1)}, u32[]{:S(2)}, u32[]{:S(2)}) collective-permute-start(bf16[1,1,4,192,256]{4,3,2,1,0:T(8,128)(2,1)S(1)} %get-tuple-element.4), channel_id=1, source_target_pairs={{0,4},{4,8},{8,12},{12,16},{16,20},{20,24},{24,28},{28,32},{32,36}... | collective-permute-start | bytes 1179656 | tf_op jit(solution)/shard_map/ppermute | solution.py:15
  78.1 2.2 %collective-permute-start.5 = (bf16[1,1,4,192,256]{4,3,2,1,0:T(8,128)(2,1)S(1)}, bf16[1,1,4,192,256]{4,3,2,1,0:T(8,128)(2,1)S(1)}, u32[]{:S(2)}, u32[]{:S(2)}) collective-permute-start(bf16[1,1,4,192,256]{4,3,2,1,0:T(8,128)(2,1)S(1)} %get-tuple-element.4), channel_id=1, source_target_pairs={{4,0},{8,4},{12,8},{16,12},{20,16},{24,20},{28,24},{32,28},{36,32}... | collective-permute-start | bytes 1179656 | tf_op jit(solution)/shard_map/ppermute | solution.py:17
  80.3 3.2 %collective-permute-done.4 = bf16[1,1,4,192,256]{4,3,2,1,0:T(8,128)(2,1)S(1)} collective-permute-done((bf16[1,1,4,192,256]{4,3,2,1,0:T(8,128)(2,1)S(1)}, bf16[1,1,4,192,256]{4,3,2,1,0:T(8,128)(2,1)S(1)}, u32[]{:S(2)}, u32[]{:S(2)}) %collective-permute-start.4) | collective-permute-done | bytes 393248 | tf_op jit(solution)/shard_map/ppermute | solution.py:15
  83.5 8.8 %collective-permute-done.5 = bf16[1,1,4,192,256]{4,3,2,1,0:T(8,128)(2,1)S(1)} collective-permute-done((bf16[1,1,4,192,256]{4,3,2,1,0:T(8,128)(2,1)S(1)}, bf16[1,1,4,192,256]{4,3,2,1,0:T(8,128)(2,1)S(1)}, u32[]{:S(2)}, u32[]{:S(2)}) %collective-permute-start.5) | collective-permute-done | bytes 393248 | tf_op jit(solution)/shard_map/ppermute | solution.py:17
  92.4 0.1 pad_maximum_fusion.1
  92.5 3.8 %collective-permute-start.6 = (bf16[3,1,4,192,256]{4,3,2,1,0:T(8,128)(2,1)S(1)}, bf16[3,1,4,192,256]{4,3,2,1,0:T(8,128)(2,1)S(1)}, u32[]{:S(2)}, u32[]{:S(2)}) collective-permute-start(bf16[3,1,4,192,256]{4,3,2,1,0:T(8,128)(2,1)S(1)} %pad_maximum_fusion.1), channel_id=1, source_target_pairs={{0,1},{1,2},{2,3},{4,5},{5,6},{6,7},{8,9},{9,10},{10,11},{12,13},{... | collective-permute-start | bytes 3538952 | tf_op jit(solution)/shard_map/ppermute | solution.py:15
  96.3 1.9 collective-permute-start.7
  98.3 11.2 %collective-permute-done.6 = bf16[3,1,4,192,256]{4,3,2,1,0:T(8,128)(2,1)S(1)} collective-permute-done((bf16[3,1,4,192,256]{4,3,2,1,0:T(8,128)(2,1)S(1)}, bf16[3,1,4,192,256]{4,3,2,1,0:T(8,128)(2,1)S(1)}, u32[]{:S(2)}, u32[]{:S(2)}) %collective-permute-start.6) | collective-permute-done | bytes 1179680 | tf_op jit(solution)/shard_map/ppermute | solution.py:15
  109.4 4.4 %collective-permute-done.7 = bf16[3,1,4,192,256]{4,3,2,1,0:T(8,128)(2,1)S(1)} collective-permute-done((bf16[3,1,4,192,256]{4,3,2,1,0:T(8,128)(2,1)S(1)}, bf16[3,1,4,192,256]{4,3,2,1,0:T(8,128)(2,1)S(1)}, u32[]{:S(2)}, u32[]{:S(2)}) %collective-permute-start.7) | collective-permute-done | bytes 1179680 | tf_op jit(solution)/shard_map/ppermute | solution.py:17
  113.8 3.2 %select_maximum_fusion.4 = bf16[3,3,6,192,256]{4,3,2,1,0:T(8,128)(2,1)} fusion(bf16[3,1,4,192,256]{4,3,2,1,0:T(8,128)(2,1)S(1)} %collective-permute-done.7, bf16[3,1,4,192,256]{4,3,2,1,0:T(8,128)(2,1)S(1)} %collective-permute-done.6, bf16[1,1,4,192,256]{4,3,2,1,0:T(8,128)(2,1)S(1)} %collective-permute-done.5, ...), kind=kLoop, calls=%fused_computation.17 | loop fusion | flops 47775744 | bytes 8847360 | tf_op jit(solution)/shard_map/concatenate | solution.py:13
  117.0 10.3 %gather_fusion.1 = bf16[104,192,256]{2,1,0:T(8,128)(2,1)} fusion(bf16[54,192,256]{2,1,0:T(8,128)(2,1)} %bitcast.119, s32[1024]{0:T(1024)S(1)} %pad_clamp_fusion.1), kind=kCustom, calls=%fused_computation.1 | custom fusion | bytes 20447648 | tf_op jit(solution)/shard_map/gather | solution.py:43
  127.3 10.0 %fusion.18 = f32[4,256,192]{1,2,0:T(8,128)S(1)} fusion(bf16[4,26,192,256]{3,2,1,0:T(8,128)(2,1)} %bitcast.122, bf16[1,1,4,26,192,192]{5,4,3,2,1,0:T(8,128)(2,1)} %param.8), kind=kOutput, calls=%fused_computation.35 | convolution fusion | flops 1962934272 | bytes 18677760 | tf_op jit(solution)/shard_map/xsij,xsjn->xin/dot_general | solution.py:44
  137.3 0.0 copy-start.5
  137.3 1.6 fusion.38
  138.9 1.9 collective-permute-start.8
  140.8 4.9 %collective-permute-start.9 = (bf16[1,1,4,192,256]{4,3,2,1,0:T(8,128)(2,1)S(1)}, bf16[1,1,4,192,256]{4,3,2,1,0:T(8,128)(2,1)S(1)}, u32[]{:S(2)}, u32[]{:S(2)}) collective-permute-start(bf16[1,1,4,192,256]{4,3,2,1,0:T(8,128)(2,1)S(1)} %get-tuple-element.2), channel_id=1, source_target_pairs={{4,0},{8,4},{12,8},{16,12},{20,16},{24,20},{28,24},{32,28},{36,32}... | collective-permute-start | bytes 1179656 | tf_op jit(solution)/shard_map/ppermute | solution.py:17
  145.7 3.2 %collective-permute-done.8 = bf16[1,1,4,192,256]{4,3,2,1,0:T(8,128)(2,1)S(1)} collective-permute-done((bf16[1,1,4,192,256]{4,3,2,1,0:T(8,128)(2,1)S(1)}, bf16[1,1,4,192,256]{4,3,2,1,0:T(8,128)(2,1)S(1)}, u32[]{:S(2)}, u32[]{:S(2)}) %collective-permute-start.8) | collective-permute-done | bytes 393248 | tf_op jit(solution)/shard_map/ppermute | solution.py:15
  148.9 6.2 %collective-permute-done.9 = bf16[1,1,4,192,256]{4,3,2,1,0:T(8,128)(2,1)S(1)} collective-permute-done((bf16[1,1,4,192,256]{4,3,2,1,0:T(8,128)(2,1)S(1)}, bf16[1,1,4,192,256]{4,3,2,1,0:T(8,128)(2,1)S(1)}, u32[]{:S(2)}, u32[]{:S(2)}) %collective-permute-start.9) | collective-permute-done | bytes 393248 | tf_op jit(solution)/shard_map/ppermute | solution.py:17
  155.1 1.1 pad_maximum_fusion.2
  156.2 2.8 %collective-permute-start.10 = (bf16[3,1,4,192,256]{4,3,2,1,0:T(8,128)(2,1)}, bf16[3,1,4,192,256]{4,3,2,1,0:T(8,128)(2,1)S(1)}, u32[]{:S(2)}, u32[]{:S(2)}) collective-permute-start(bf16[3,1,4,192,256]{4,3,2,1,0:T(8,128)(2,1)} %pad_maximum_fusion.2), channel_id=1, source_target_pairs={{0,1},{1,2},{2,3},{4,5},{5,6},{6,7},{8,9},{9,10},{10,11},{12,13},{... | collective-permute-start | bytes 3538952 | tf_op jit(solution)/shard_map/ppermute | solution.py:15
  159.1 2.1 %collective-permute-start.11 = (bf16[3,1,4,192,256]{4,3,2,1,0:T(8,128)(2,1)}, bf16[3,1,4,192,256]{4,3,2,1,0:T(8,128)(2,1)}, u32[]{:S(2)}, u32[]{:S(2)}) collective-permute-start(bf16[3,1,4,192,256]{4,3,2,1,0:T(8,128)(2,1)} %pad_maximum_fusion.2), channel_id=1, source_target_pairs={{1,0},{2,1},{3,2},{5,4},{6,5},{7,6},{9,8},{10,9},{11,10},{13,12},{... | collective-permute-start | bytes 3538952 | tf_op jit(solution)/shard_map/ppermute | solution.py:17
  161.2 0.6 gather_fusion.2
  161.8 10.7 %collective-permute-done.10 = bf16[3,1,4,192,256]{4,3,2,1,0:T(8,128)(2,1)S(1)} collective-permute-done((bf16[3,1,4,192,256]{4,3,2,1,0:T(8,128)(2,1)}, bf16[3,1,4,192,256]{4,3,2,1,0:T(8,128)(2,1)S(1)}, u32[]{:S(2)}, u32[]{:S(2)}) %collective-permute-start.10) | collective-permute-done | bytes 1179680 | tf_op jit(solution)/shard_map/ppermute | solution.py:15
  172.5 4.4 %collective-permute-done.11 = bf16[3,1,4,192,256]{4,3,2,1,0:T(8,128)(2,1)} collective-permute-done((bf16[3,1,4,192,256]{4,3,2,1,0:T(8,128)(2,1)}, bf16[3,1,4,192,256]{4,3,2,1,0:T(8,128)(2,1)}, u32[]{:S(2)}, u32[]{:S(2)}) %collective-permute-start.11) | collective-permute-done | bytes 1179680 | tf_op jit(solution)/shard_map/ppermute | solution.py:17
  176.9 4.1 %select_maximum_fusion = bf16[3,3,6,192,256]{4,3,2,1,0:T(8,128)(2,1)} fusion(bf16[3,1,4,192,256]{4,3,2,1,0:T(8,128)(2,1)} %collective-permute-done.11, bf16[3,1,4,192,256]{4,3,2,1,0:T(8,128)(2,1)S(1)} %collective-permute-done.10, bf16[1,1,4,192,256]{4,3,2,1,0:T(8,128)(2,1)S(1)} %collective-permute-done.9, ...), kind=kLoop, calls=%fused_computation.13 | loop fusion | flops 47775744 | bytes 8847360 | tf_op jit(solution)/shard_map/concatenate | solution.py:13
  181.0 10.3 %gather_fusion.3 = bf16[104,192,256]{2,1,0:T(8,128)(2,1)} fusion(bf16[54,192,256]{2,1,0:T(8,128)(2,1)} %bitcast.118, s32[1024]{0:T(1024)S(1)} %pad_clamp_fusion.1), kind=kCustom, calls=%fused_computation.3 | custom fusion | bytes 20447648 | tf_op jit(solution)/shard_map/gather | solution.py:43
  191.3 10.0 %fusion.15 = f32[4,256,192]{1,2,0:T(8,128)} fusion(bf16[4,26,192,256]{3,2,1,0:T(8,128)(2,1)} %bitcast.120, bf16[1,1,4,26,192,192]{5,4,3,2,1,0:T(8,128)(2,1)} %param.8), kind=kOutput, calls=%fused_computation.34 | convolution fusion | flops 1962934272 | bytes 18677760 | tf_op jit(solution)/shard_map/xsij,xsjn->xin/dot_general | solution.py:44
  201.3 1.6 bitcast_reduce_fusion
  203.0 0.1 collective-permute-start.12
  203.1 5.0 %collective-permute-done.12 = bf16[1,192,256]{2,1,0:T(8,128)(2,1)S(1)} collective-permute-done((bf16[1,192,256]{2,1,0:T(8,128)(2,1)S(1)}, bf16[1,192,256]{2,1,0:T(8,128)(2,1)S(1)}, u32[]{:S(2)}, u32[]{:S(2)}) %collective-permute-start.12) | collective-permute-done | bytes 98336 | tf_op jit(solution)/shard_map/ppermute | solution.py:27
  208.0 0.7 fusion.39
  (14 shorter events, 0.1 us)
Async XLA Ops:
  0.6 160.6 %copy-start = (bf16[8,192,192]{2,1,0:T(8,128)(2,1)S(1)}, bf16[8,192,192]{2,1,0:T(8,128)(2,1)}, u32[]{:S(2)}) copy-start(bf16[8,192,192]{2,1,0:T(8,128)(2,1)} %param.12) | copy-start | bytes 1769476
  2.6 13.4 %collective-permute-start = (bf16[1,1,4,192,256]{4,3,2,1,0:T(8,128)(2,1)S(1)}, bf16[1,1,4,192,256]{4,3,2,1,0:T(8,128)(2,1)S(1)}, u32[]{:S(2)}, u32[]{:S(2)}) collective-permute-start(bf16[1,1,4,192,256]{4,3,2,1,0:T(8,128)(2,1)S(1)} %fusion.49), channel_id=1, source_target_pairs={{0,4},{4,8},{8,12},{12,16},{16,20},{20,24},{24,28},{28,32},{32,36}... | collective-permute-start | bytes 1179656 | tf_op jit(solution)/shard_map/ppermute | solution.py:15
  6.9 17.3 %collective-permute-start.1 = (bf16[1,1,4,192,256]{4,3,2,1,0:T(8,128)(2,1)S(1)}, bf16[1,1,4,192,256]{4,3,2,1,0:T(8,128)(2,1)S(1)}, u32[]{:S(2)}, u32[]{:S(2)}) collective-permute-start(bf16[1,1,4,192,256]{4,3,2,1,0:T(8,128)(2,1)S(1)} %fusion.49), channel_id=1, source_target_pairs={{4,0},{8,4},{12,8},{16,12},{20,16},{24,20},{28,24},{32,28},{36,32}... | collective-permute-start | bytes 1179656 | tf_op jit(solution)/shard_map/ppermute | solution.py:17
  25.4 18.9 %collective-permute-start.2 = (bf16[3,1,4,192,256]{4,3,2,1,0:T(8,128)(2,1)}, bf16[3,1,4,192,256]{4,3,2,1,0:T(8,128)(2,1)S(1)}, u32[]{:S(2)}, u32[]{:S(2)}) collective-permute-start(bf16[3,1,4,192,256]{4,3,2,1,0:T(8,128)(2,1)} %pad_maximum_fusion), channel_id=1, source_target_pairs={{0,1},{1,2},{2,3},{4,5},{5,6},{6,7},{8,9},{9,10},{10,11},{12,13},{... | collective-permute-start | bytes 3538952 | tf_op jit(solution)/shard_map/ppermute | solution.py:15
  30.8 17.8 %collective-permute-start.3 = (bf16[3,1,4,192,256]{4,3,2,1,0:T(8,128)(2,1)}, bf16[3,1,4,192,256]{4,3,2,1,0:T(8,128)(2,1)}, u32[]{:S(2)}, u32[]{:S(2)}) collective-permute-start(bf16[3,1,4,192,256]{4,3,2,1,0:T(8,128)(2,1)} %pad_maximum_fusion), channel_id=1, source_target_pairs={{1,0},{2,1},{3,2},{5,4},{6,5},{7,6},{9,8},{10,9},{11,10},{13,12},{... | collective-permute-start | bytes 3538952 | tf_op jit(solution)/shard_map/ppermute | solution.py:17
  63.0 10.1 %copy-start.1 = (f32[1,1,4,192,256]{4,3,2,1,0:T(8,128)S(1)}, f32[1,1,4,192,256]{4,3,2,1,0:T(8,128)}, u32[]{:S(2)}) copy-start(f32[1,1,4,192,256]{4,3,2,1,0:T(8,128)} %param.7) | copy-start | bytes 2359300
  63.0 10.1 %copy-start.3 = (bf16[1,1,4,192,192]{4,3,2,1,0:T(8,128)(2,1)S(1)}, bf16[1,1,4,192,192]{4,3,2,1,0:T(8,128)(2,1)}, u32[]{:S(2)}) copy-start(bf16[1,1,4,192,192]{4,3,2,1,0:T(8,128)(2,1)} %param.9) | copy-start | bytes 884740
  73.5 10.0 %collective-permute-start.4 = (bf16[1,1,4,192,256]{4,3,2,1,0:T(8,128)(2,1)S(1)}, bf16[1,1,4,192,256]{4,3,2,1,0:T(8,128)(2,1)S(1)}, u32[]{:S(2)}, u32[]{:S(2)}) collective-permute-start(bf16[1,1,4,192,256]{4,3,2,1,0:T(8,128)(2,1)S(1)} %get-tuple-element.4), channel_id=1, source_target_pairs={{0,4},{4,8},{8,12},{12,16},{16,20},{20,24},{24,28},{28,32},{32,36}... | collective-permute-start | bytes 1179656 | tf_op jit(solution)/shard_map/ppermute | solution.py:15
  78.1 14.2 %collective-permute-start.5 = (bf16[1,1,4,192,256]{4,3,2,1,0:T(8,128)(2,1)S(1)}, bf16[1,1,4,192,256]{4,3,2,1,0:T(8,128)(2,1)S(1)}, u32[]{:S(2)}, u32[]{:S(2)}) collective-permute-start(bf16[1,1,4,192,256]{4,3,2,1,0:T(8,128)(2,1)S(1)} %get-tuple-element.4), channel_id=1, source_target_pairs={{4,0},{8,4},{12,8},{16,12},{20,16},{24,20},{28,24},{32,28},{36,32}... | collective-permute-start | bytes 1179656 | tf_op jit(solution)/shard_map/ppermute | solution.py:17
  92.5 16.9 %collective-permute-start.6 = (bf16[3,1,4,192,256]{4,3,2,1,0:T(8,128)(2,1)S(1)}, bf16[3,1,4,192,256]{4,3,2,1,0:T(8,128)(2,1)S(1)}, u32[]{:S(2)}, u32[]{:S(2)}) collective-permute-start(bf16[3,1,4,192,256]{4,3,2,1,0:T(8,128)(2,1)S(1)} %pad_maximum_fusion.1), channel_id=1, source_target_pairs={{0,1},{1,2},{2,3},{4,5},{5,6},{6,7},{8,9},{9,10},{10,11},{12,13},{... | collective-permute-start | bytes 3538952 | tf_op jit(solution)/shard_map/ppermute | solution.py:15
  96.3 17.5 %collective-permute-start.7 = (bf16[3,1,4,192,256]{4,3,2,1,0:T(8,128)(2,1)S(1)}, bf16[3,1,4,192,256]{4,3,2,1,0:T(8,128)(2,1)S(1)}, u32[]{:S(2)}, u32[]{:S(2)}) collective-permute-start(bf16[3,1,4,192,256]{4,3,2,1,0:T(8,128)(2,1)S(1)} %pad_maximum_fusion.1), channel_id=1, source_target_pairs={{1,0},{2,1},{3,2},{5,4},{6,5},{7,6},{9,8},{10,9},{11,10},{13,12},{... | collective-permute-start | bytes 3538952 | tf_op jit(solution)/shard_map/ppermute | solution.py:17
  137.3 23.9 %copy-start.5 = (s32[1,1,4]{2,1,0:T(1,128)S(1)}, s32[1,1,4]{2,1,0:T(1,128)}, u32[]{:S(2)}) copy-start(s32[1,1,4]{2,1,0:T(1,128)} %param.13) | copy-start | bytes 52
  138.9 10.0 %collective-permute-start.8 = (bf16[1,1,4,192,256]{4,3,2,1,0:T(8,128)(2,1)S(1)}, bf16[1,1,4,192,256]{4,3,2,1,0:T(8,128)(2,1)S(1)}, u32[]{:S(2)}, u32[]{:S(2)}) collective-permute-start(bf16[1,1,4,192,256]{4,3,2,1,0:T(8,128)(2,1)S(1)} %get-tuple-element.2), channel_id=1, source_target_pairs={{0,4},{4,8},{8,12},{12,16},{16,20},{20,24},{24,28},{28,32},{32,36}... | collective-permute-start | bytes 1179656 | tf_op jit(solution)/shard_map/ppermute | solution.py:15
  140.8 14.3 %collective-permute-start.9 = (bf16[1,1,4,192,256]{4,3,2,1,0:T(8,128)(2,1)S(1)}, bf16[1,1,4,192,256]{4,3,2,1,0:T(8,128)(2,1)S(1)}, u32[]{:S(2)}, u32[]{:S(2)}) collective-permute-start(bf16[1,1,4,192,256]{4,3,2,1,0:T(8,128)(2,1)S(1)} %get-tuple-element.2), channel_id=1, source_target_pairs={{4,0},{8,4},{12,8},{16,12},{20,16},{24,20},{28,24},{32,28},{36,32}... | collective-permute-start | bytes 1179656 | tf_op jit(solution)/shard_map/ppermute | solution.py:17
  156.2 16.3 %collective-permute-start.10 = (bf16[3,1,4,192,256]{4,3,2,1,0:T(8,128)(2,1)}, bf16[3,1,4,192,256]{4,3,2,1,0:T(8,128)(2,1)S(1)}, u32[]{:S(2)}, u32[]{:S(2)}) collective-permute-start(bf16[3,1,4,192,256]{4,3,2,1,0:T(8,128)(2,1)} %pad_maximum_fusion.2), channel_id=1, source_target_pairs={{0,1},{1,2},{2,3},{4,5},{5,6},{6,7},{8,9},{9,10},{10,11},{12,13},{... | collective-permute-start | bytes 3538952 | tf_op jit(solution)/shard_map/ppermute | solution.py:15
  159.1 17.8 %collective-permute-start.11 = (bf16[3,1,4,192,256]{4,3,2,1,0:T(8,128)(2,1)}, bf16[3,1,4,192,256]{4,3,2,1,0:T(8,128)(2,1)}, u32[]{:S(2)}, u32[]{:S(2)}) collective-permute-start(bf16[3,1,4,192,256]{4,3,2,1,0:T(8,128)(2,1)} %pad_maximum_fusion.2), channel_id=1, source_target_pairs={{1,0},{2,1},{3,2},{5,4},{6,5},{7,6},{9,8},{10,9},{11,10},{13,12},{... | collective-permute-start | bytes 3538952 | tf_op jit(solution)/shard_map/ppermute | solution.py:17
  191.3 10.0 %copy-start.2 = (f32[1,1,4,192,256]{4,3,2,1,0:T(8,128)S(1)}, f32[1,1,4,192,256]{4,3,2,1,0:T(8,128)}, u32[]{:S(2)}) copy-start(f32[1,1,4,192,256]{4,3,2,1,0:T(8,128)} %get-tuple-element.6) | copy-start | bytes 2359300
  191.3 10.0 %copy-start.4 = (bf16[1,1,4,192,192]{4,3,2,1,0:T(8,128)(2,1)S(1)}, bf16[1,1,4,192,192]{4,3,2,1,0:T(8,128)(2,1)}, u32[]{:S(2)}) copy-start(bf16[1,1,4,192,192]{4,3,2,1,0:T(8,128)(2,1)} %param.9) | copy-start | bytes 884740
  203.0 5.1 %collective-permute-start.12 = (bf16[1,192,256]{2,1,0:T(8,128)(2,1)S(1)}, bf16[1,192,256]{2,1,0:T(8,128)(2,1)S(1)}, u32[]{:S(2)}, u32[]{:S(2)}) collective-permute-start(bf16[1,192,256]{2,1,0:T(8,128)(2,1)S(1)} %fusion.41), channel_id=1, source_target_pairs={{0,4},{4,0},{8,12},{12,8},{16,20},{20,16},{24,28},{28,24},{32,36},... | collective-permute-start | bytes 294920 | tf_op jit(solution)/shard_map/ppermute | solution.py:27
where the time goes:
time: 209 us
  waiting for transfers between devices  87 us (42%)
  starting transfers between devices  38.5 us (18%)
  matrix products  33.7 us (16%)
  local copies, waits for them, and re-layouts  31.5 us (15%)
  other arithmetic  16.4 us (8%)
    ppermute x6, waiting for transfers between devices, extended(): lax.ppermute(tail, axis, [(i, (i + 1) % count) for i in range(ends)])  45.5 us
    ppermute x6, waiting for transfers between devices, extended(): lax.ppermute(head, axis, [((i + 1) % count, i) for i in range(ends)])  36.5 us
    gather x3, local copies, waits for them, and re-layouts, apply_local(): gathered = flat[flat_index]  30.8 us
    dot_general x3, matrix products, apply_local(): jnp.einsum('xsij,xsjn->xin', blocks[0, 0], gathered, preferred_element_ty...  30.1 us
    ppermute x6, starting transfers between devices, extended(): lax.ppermute(tail, axis, [(i, (i + 1) % count) for i in range(ends)])  23 us
    ppermute x6, starting transfers between devices, extended(): lax.ppermute(head, axis, [((i + 1) % count, i) for i in range(ends)])  15.4 us
    concatenate x6, other arithmetic, extended(): jnp.concatenate([lax.ppermute(tail, axis, [(i, (i + 1) % count) for i in...  13.8 us
    ppermute x1, waiting for transfers between devices, from_partner(): return lax.ppermute(value, axis, pairs)  4.96 us
  transfers between devices with their start and end apart: 13, of which 13 were waited for; matrix products, arithmetic and copies ran while one was open for 1% of the time, Pallas kernels for 0%

commit v1 on v0

v1 whole, which is shorter than its diff:
```python
import functools

import jax
import jax.numpy as jnp
from jax import lax
from jax.experimental import pallas as pl
from jax.experimental.pallas import tpu as pltpu
from jax.sharding import PartitionSpec as P

OWN, NEAR, FAR = 0, 1, 2
SELF, SIB, CROSS = 0, 1, 2
ROUNDS = 3
HALVES = 2
MESH = pl.DeviceIdType.MESH
F32 = jnp.float32
BF16 = jnp.bfloat16


def smooth_kernel(
    layers,
    slot_ref,
    kind_ref,
    bound_ref,
    rhs_hbm,
    blocks_hbm,
    diag_hbm,
    restrict_hbm,
    smoothed_hbm,
    coarse_hbm,
    oper,
    halo,
    residual,
    direction,
    smoothed,
    restrict,
    kept,
    leaving,
    arrived,
    load_sem,
    send_sem,
    recv_sem,
    coarse_sem,
):
    s = lax.axis_index("slab")
    q = lax.axis_index("quad")
    parity = lax.rem(s, 2)
    inner = (q == 1) | (q == 2)
    near_s = s + 1 - 2 * parity
    step = 2 - 4 * parity
    sibling = (s, q + 1 - 2 * lax.rem(q, 2))
    across = (s, 3 - q)
    diagonal = (near_s, 3 - q)
    opposite = (near_s, q)
    ahead = (lax.rem(s + step + layers, layers), q)
    behind = (lax.rem(s - step + layers, layers), q)
    dz_near = 2 - 2 * parity
    dy_sib = 2 - 2 * lax.rem(q, 2)
    has_far = jnp.where(parity == 0, s > 0, s < layers - 1)
    xb, width, cols = residual.shape
    half = cols // HALVES
    slots = blocks_hbm.shape[1]

    load_rhs = pltpu.make_async_copy(rhs_hbm, residual, load_sem.at[0])
    load_diag = pltpu.make_async_copy(diag_hbm, oper.at[:, slots], load_sem.at[1])
    load_blocks = [
        pltpu.make_async_copy(blocks_hbm.at[x], oper.at[x, pl.ds(0, slots)], load_sem.at[2 + x]) for x in range(xb)
    ]
    load_restrict = pltpu.make_async_copy(restrict_hbm, restrict, load_sem.at[2 + xb])
    load_rhs.start()
    load_diag.start()
    for load in load_blocks:
        load.start()
    load_restrict.start()

    def copy(k, h, r, lane, src, dst, device):
        return pltpu.make_async_remote_copy(
            src_ref=halo.at[r, h, src[0], src[1]],
            dst_ref=halo.at[r, h, dst[0], dst[1]],
            send_sem=send_sem.at[r, h, lane],
            recv_sem=recv_sem.at[r, h, dst[0] * 3 + dst[1]],
            device_id=device,
            device_id_type=MESH,
        )

    def own_to_sib(r, h):
        return copy(0, h, r, 0, (OWN, SELF), (OWN, SIB), sibling)

    def own_to_across(r, h):
        return copy(0, h, r, 1, (OWN, SELF), (OWN, CROSS), across)

    def own_to_diagonal(r, h):
        return copy(0, h, r, 2, (OWN, SELF), (NEAR, CROSS), diagonal)

    def relay(r, h):
        if h == 0:
            return copy(0, h, r, 3, (OWN, CROSS), (NEAR, SELF), diagonal)
        return copy(0, h, r, 3, (NEAR, CROSS), (NEAR, SELF), across)

    def near_to_sib(r, h):
        return copy(0, h, r, 4, (NEAR, SELF), (NEAR, SIB), sibling)

    def near_to_ahead(r, h):
        return copy(0, h, r, 5, (NEAR, SELF), (FAR, SELF), ahead)

    def cross_to_ahead(r, h):
        return copy(0, h, r, 6, (NEAR, CROSS), (FAR, CROSS), ahead)

    def far_to_sib(r, h):
        return copy(0, h, r, 7, (FAR, SELF), (FAR, SIB), sibling)

    def await_piece(r, h, a, b):
        copy(0, h, r, 0, (a, b), (a, b), sibling).wait_recv()

    def send_own(r):
        own_to_across(r, 0).start()
        own_to_diagonal(r, 1).start()

        @pl.when(inner)
        def _():
            own_to_diagonal(r, 0).start()
            own_to_across(r, 1).start()

        own_to_sib(r, 0).start()
        own_to_sib(r, 1).start()

    def apply(r, a, b):
        dz = (1, dz_near, 2 - dz_near)[a]
        dy = (1, dy_sib, 2 - dy_sib)[b]
        base = dz * 9 + dy * 3
        for source in range(xb):
            targets = [x for x in (source - 1, source, source + 1) if 0 <= x < xb]
            rows = [oper[x, slot_ref[x, base + source - x + 1]] for x in targets]
            column = jnp.concatenate([halo[r, h, a, b, source] for h in range(HALVES)], axis=1)
            moved = jnp.dot(jnp.concatenate(rows, axis=0), column, preferred_element_type=F32)
            for i, x in enumerate(targets):
                residual[x] -= moved[i * width : (i + 1) * width]

    bound = bound_ref[0]
    sigma = 9.0 / 7.0
    theta = 9.0 * bound / 16.0
    delta = 7.0 * bound / 16.0
    rho_0 = 1.0 / sigma
    rho_1 = 1.0 / (2.0 * sigma - rho_0)
    rho_2 = 1.0 / (2.0 * sigma - rho_1)

    barrier = pltpu.get_barrier_semaphore()
    for device in (sibling, across, diagonal, opposite, ahead, behind):
        pl.semaphore_signal(barrier, inc=1, device_id=device, device_id_type=MESH)

    load_rhs.wait()

    def first_direction(x, carry):
        value = residual[x] / theta
        direction[x] = value
        smoothed[x] = value
        for h in range(HALVES):
            halo[0, h, OWN, SELF, x] = value[:, h * half : (h + 1) * half].astype(BF16)
        return carry

    lax.fori_loop(0, xb, first_direction, 0)
    pl.semaphore_wait(barrier, 6)
    send_own(0)
    load_diag.wait()
    for load in load_blocks:
        load.wait()
    load_restrict.wait()

    def one_round(r, carry):
        apply(r, OWN, SELF)
        await_piece(r, 0, OWN, CROSS)
        relay(r, 0).start()
        await_piece(r, 1, NEAR, CROSS)
        relay(r, 1).start()

        @pl.when(inner)
        def _():
            cross_to_ahead(r, 1).start()
            await_piece(r, 0, NEAR, CROSS)
            cross_to_ahead(r, 0).start()
            await_piece(r, 1, OWN, CROSS)

        for h in range(HALVES):
            await_piece(r, h, OWN, SIB)
        apply(r, OWN, SIB)
        for h in range(HALVES):
            await_piece(r, h, NEAR, SELF)
            near_to_ahead(r, h).start()
            near_to_sib(r, h).start()

        @pl.when(inner)
        def _():
            apply(r, OWN, CROSS)
            apply(r, NEAR, CROSS)

        apply(r, NEAR, SELF)
        for h in range(HALVES):
            await_piece(r, h, NEAR, SIB)
        apply(r, NEAR, SIB)

        for h in range(HALVES):
            await_piece(r, h, FAR, SELF)
            far_to_sib(r, h).start()

        @pl.when(inner)
        def _():
            for h in range(HALVES):
                await_piece(r, h, FAR, CROSS)

        @pl.when(inner & has_far)
        def _():
            apply(r, FAR, CROSS)

        @pl.when(has_far)
        def _():
            apply(r, FAR, SELF)

        for h in range(HALVES):
            await_piece(r, h, FAR, SIB)

        @pl.when(has_far)
        def _():
            apply(r, FAR, SIB)

        @pl.when(r < ROUNDS - 1)
        def _():
            scale = jnp.where(r == 0, rho_1 * rho_0, rho_2 * rho_1)
            gain = jnp.where(r == 0, 2.0 * rho_1 / delta, 2.0 * rho_2 / delta)

            def next_direction(x, carry):
                value = scale * direction[x] + gain * residual[x]
                direction[x] = value
                smoothed[x] += value
                for h in range(HALVES):
                    halo[r + 1, h, OWN, SELF, x] = value[:, h * half : (h + 1) * half].astype(BF16)
                return carry

            lax.fori_loop(0, xb, next_direction, 0)
            send_own(r + 1)

        return carry

    lax.fori_loop(0, ROUNDS, one_round, 0)

    store_smoothed = pltpu.make_async_copy(smoothed, smoothed_hbm, load_sem.at[0])
    store_smoothed.start()

    def restricted(pair):
        total = None
        for i in range(2):
            x = 2 * pair + i
            term = jnp.dot(restrict[kind_ref[x]], residual[x].astype(BF16), preferred_element_type=F32)
            total = term if total is None else total + term
        return total

    leaving[...] = restricted(1 - parity).astype(BF16)
    hand_over = pltpu.make_async_remote_copy(
        src_ref=leaving,
        dst_ref=arrived,
        send_sem=coarse_sem.at[0],
        recv_sem=coarse_sem.at[1],
        device_id=opposite,
        device_id_type=MESH,
    )
    hand_over.start()
    kept[...] = restricted(parity)

    def drain(r, carry):
        for h in range(HALVES):
            own_to_sib(r, h).wait_send()
            relay(r, h).wait_send()
            near_to_sib(r, h).wait_send()
            near_to_ahead(r, h).wait_send()
            far_to_sib(r, h).wait_send()
        own_to_across(r, 0).wait_send()
        own_to_diagonal(r, 1).wait_send()

        @pl.when(inner)
        def _():
            own_to_across(r, 1).wait_send()
            own_to_diagonal(r, 0).wait_send()
            for h in range(HALVES):
                cross_to_ahead(r, h).wait_send()

        return carry

    lax.fori_loop(0, ROUNDS, drain, 0)
    hand_over.wait()
    kept[...] += arrived[...].astype(F32)
    store_coarse = pltpu.make_async_copy(kept, coarse_hbm, load_sem.at[1])
    store_coarse.start()
    store_coarse.wait()
    store_smoothed.wait()


def on_device(layers, rhs, blocks, diag_blocks, neighbours, bound, restrict_blocks, restrict_kind):
    xb, width, cols = rhs.shape[2:]
    slots = blocks.shape[3]
    codes = neighbours[0, 0]
    codes = codes + (codes >= slots // 2).astype(jnp.int32)
    names = jnp.arange(slots + 1, dtype=jnp.int32)
    order = jnp.arange(slots, dtype=jnp.int32)
    slot_of = jnp.sum(jnp.where(codes[:, :, None] == names, order[:, None] - slots, 0), axis=1) + slots
    half = cols // HALVES
    smem = pl.BlockSpec(memory_space=pltpu.SMEM)
    hbm = pl.BlockSpec(memory_space=pl.ANY)
    smoothed, coarse = pl.pallas_call(
        functools.partial(smooth_kernel, layers),
        out_shape=(
            jax.ShapeDtypeStruct((xb, width, cols), F32),
            jax.ShapeDtypeStruct((width, cols), F32),
        ),
        in_specs=[smem, smem, smem, hbm, hbm, hbm, hbm],
        out_specs=(hbm, hbm),
        scratch_shapes=[
            pltpu.VMEM((xb, slots + 1, width, width), BF16),
            pltpu.VMEM((ROUNDS, HALVES, 3, 3, xb, width, half), BF16),
            pltpu.VMEM((xb, width, cols), F32),
            pltpu.VMEM((xb, width, cols), F32),
            pltpu.VMEM((xb, width, cols), F32),
            pltpu.VMEM(restrict_blocks.shape, BF16),
            pltpu.VMEM((width, cols), F32),
            pltpu.VMEM((width, cols), BF16),
            pltpu.VMEM((width, cols), BF16),
            pltpu.SemaphoreType.DMA((3 + xb,)),
            pltpu.SemaphoreType.DMA((ROUNDS, HALVES, 8)),
            pltpu.SemaphoreType.DMA((ROUNDS, HALVES, 9)),
            pltpu.SemaphoreType.DMA((2,)),
        ],
        compiler_params=pltpu.CompilerParams(
            collective_id=0, has_side_effects=True, vmem_limit_bytes=56 * 2**20
        ),
        cost_estimate=pl.CostEstimate(flops=6 * 10**9, bytes_accessed=11 * 10**6, transcendentals=0),
        name="smooth_and_restrict",
    )(slot_of, restrict_kind[0, 0], bound, rhs[0, 0], blocks[0, 0], diag_blocks[0, 0], restrict_blocks)
    return smoothed[None, None], coarse[None, None, None]


def solution(mesh):
    return jax.shard_map(
        functools.partial(on_device, mesh.shape["slab"]),
        mesh=mesh,
        in_specs=(
            P("slab", "quad", None, None, None),
            P("slab", "quad", None, None, None, None),
            P("slab", "quad", None, None, None),
            P("slab", "quad", None, None),
            P(),
            P(),
            P("slab", "quad", None),
        ),
        out_specs=(P("slab", "quad", None, None, None), P("slab", "quad", None, None, None)),
        check_vma=False,
    )
```

time: 209 us -> 98.7 us (0.47)
  the two profiles are of different devices: /device:TPU:125 before, /device:TPU:5 now
where the time goes in v1:
time: 98.7 us; the launch traced here: 97.7 us
  Pallas kernels  91.3 us (93%)
  local copies, waits for them, and re-layouts  3.78 us (4%)
  other arithmetic  1.4 us (1%)
  between operations  1.3 us (1%)
    pallas_call x1, Pallas kernels, on_device(): pl.pallas_call(functools.partial(smooth_kernel, layers), out_shape=(jax.S...  91.3 us
    unnamed x2, local copies, waits for them, and re-layouts  3.68 us

profile of v1, /device:TPU:5, one launch (start us, length us, event | category | flops | bytes accessed | tf_op | source)
XLA Modules:
  0.0 97.7 jit_solution(5724914641184317977)
XLA Ops:
  1.3 0.7 bitcast_add_fusion
  2.0 0.1 copy.9
  2.1 0.1 select_reduce_fusion
  2.2 0.6 broadcast_add_fusion.slot_ref
  2.8 91.3 %smooth_and_restrict.1 = (f32[4,192,256]{2,1,0:T(8,128)}, f32[192,256]{1,0:T(8,128)}) custom-call(s32[4,27]{1,0:T(4,128)} %broadcast_add_fusion.slot_ref, s32[4]{0:T(128)} %bitcast.16, f32[1]{0:T(128)S(6)} %copy.12.bound_ref, f32[4,192,256]{2,1,0:T(8,128)} %bitcast.14, bf16[4,26,192,192]{3,2,1,0:T(8,128)(2,1)} %bitcast.13, bf16[4,192,192]{2,1,0:T(8,128)(2,1)} %bitcast.15, ...), custom_call_target="tpu_custom_call" | custom-call | flops 6000000000 | bytes 11000000 | tf_op jit(solution)/shard_map/smooth_and_restrict/pallas_call | solution.py:306
  94.1 2.1 %copy.13 = f32[1,1,4,192,256]{4,3,2,1,0:T(8,128)} copy(f32[1,1,4,192,256]{4,3,2,1,0:T(8,128)} %bitcast.11) | data formatting | bytes 1572864
  96.1 1.6 %copy.14 = f32[1,1,1,192,256]{4,3,2,1,0:T(8,128)} copy(f32[1,1,1,192,256]{4,3,2,1,0:T(8,128)} %bitcast.12) | data formatting | bytes 393216
  (1 shorter events, 0.0 us)

commit v2 on v0

v2 whole, which is shorter than its diff:
```python
import functools

import jax
import jax.numpy as jnp
from jax import lax
from jax.experimental import pallas as pl
from jax.experimental.pallas import tpu as pltpu
from jax.sharding import PartitionSpec as P

OWN, NEAR, FAR = 0, 1, 2
SELF, SIB, CROSS = 0, 1, 2
ROUNDS = 3
HALVES = 2
PIECES = 2
MESH = pl.DeviceIdType.MESH
F32 = jnp.float32
BF16 = jnp.bfloat16


def smooth_kernel(
    layers,
    slot_ref,
    kind_ref,
    bound_ref,
    rhs_hbm,
    blocks_hbm,
    diag_hbm,
    restrict_hbm,
    later_hbm,
    kept_hbm,
    arrived_hbm,
    oper,
    halo,
    residual,
    direction,
    later,
    restrict,
    kept,
    leaving,
    load_sem,
    store_sem,
    send_sem,
    recv_sem,
    coarse_sem,
):
    s = lax.axis_index("slab")
    q = lax.axis_index("quad")
    parity = lax.rem(s, 2)
    inner = (q == 1) | (q == 2)
    near_s = s + 1 - 2 * parity
    step = 2 - 4 * parity
    sibling = (s, q + 1 - 2 * lax.rem(q, 2))
    across = (s, 3 - q)
    diagonal = (near_s, 3 - q)
    opposite = (near_s, q)
    ahead = (lax.rem(s + step + layers, layers), q)
    behind = (lax.rem(s - step + layers, layers), q)
    dz_near = 2 - 2 * parity
    dy_sib = 2 - 2 * lax.rem(q, 2)
    has_far = jnp.where(parity == 0, s > 0, s < layers - 1)
    xb, width, half = residual.shape[1:]
    slots = blocks_hbm.shape[1]
    per_piece = xb // PIECES

    load_rhs = [
        pltpu.make_async_copy(rhs_hbm.at[:, :, pl.ds(h * half, half)], residual.at[h], load_sem.at[h])
        for h in range(HALVES)
    ]
    load_operator = [pltpu.make_async_copy(diag_hbm, oper.at[:, slots], load_sem.at[2])] + [
        pltpu.make_async_copy(blocks_hbm.at[x], oper.at[x, pl.ds(0, slots)], load_sem.at[3 + x]) for x in range(xb)
    ]
    load_restrict = pltpu.make_async_copy(restrict_hbm, restrict, load_sem.at[3 + xb])
    for load in load_rhs + load_operator + [load_restrict]:
        load.start()

    def copy(r, h, lane, src, dst, device, piece):
        blocks = pl.ds(piece * per_piece, per_piece)
        return pltpu.make_async_remote_copy(
            src_ref=halo.at[r, h, src[0], src[1], blocks],
            dst_ref=halo.at[r, h, dst[0], dst[1], blocks],
            send_sem=send_sem.at[r, h, lane, piece],
            recv_sem=recv_sem.at[r, h, dst[0] * 3 + dst[1], piece],
            device_id=device,
            device_id_type=MESH,
        )

    def own_to_sib(r, h, piece):
        return copy(r, h, 0, (OWN, SELF), (OWN, SIB), sibling, piece)

    def own_to_across(r, h, piece):
        return copy(r, h, 1, (OWN, SELF), (OWN, CROSS), across, piece)

    def own_to_diagonal(r, h, piece):
        return copy(r, h, 2, (OWN, SELF), (NEAR, CROSS), diagonal, piece)

    def own_to_opposite(r, h, piece):
        return copy(r, h, 3, (OWN, SELF), (NEAR, SELF), opposite, piece)

    def near_to_sib(r, h, piece):
        return copy(r, h, 4, (NEAR, SELF), (NEAR, SIB), sibling, piece)

    def near_to_ahead(r, h, piece):
        return copy(r, h, 5, (NEAR, SELF), (FAR, SELF), ahead, piece)

    def cross_to_ahead(r, h, piece):
        return copy(r, h, 6, (NEAR, CROSS), (FAR, CROSS), ahead, piece)

    def far_to_sib(r, h, piece):
        return copy(r, h, 7, (FAR, SELF), (FAR, SIB), sibling, piece)

    def await_piece(r, h, a, b, piece):
        copy(r, h, 0, (a, b), (a, b), sibling, piece).wait_recv()

    def await_row(r, h, a, b):
        for piece in range(PIECES):
            await_piece(r, h, a, b, piece)

    def send_own(r, h):
        for piece in range(PIECES):
            own_to_opposite(r, h, piece).start()

        @pl.when(inner)
        def _():
            for piece in range(PIECES):
                own_to_diagonal(r, h, piece).start()

        for piece in range(PIECES):
            own_to_sib(r, h, piece).start()

        @pl.when(inner)
        def _():
            for piece in range(PIECES):
                own_to_across(r, h, piece).start()

    def apply(r, h, a, b):
        dz = (1, dz_near, 2 - dz_near)[a]
        dy = (1, dy_sib, 2 - dy_sib)[b]
        base = dz * 9 + dy * 3
        for source in range(xb):
            targets = [x for x in (source - 1, source, source + 1) if 0 <= x < xb]
            rows = [oper[x, slot_ref[x, base + source - x + 1]] for x in targets]
            moved = jnp.dot(jnp.concatenate(rows, axis=0), halo[r, h, a, b, source], preferred_element_type=F32)
            for i, x in enumerate(targets):
                residual[h, x] -= moved[i * width : (i + 1) * width]

    bound = bound_ref[0]
    sigma = 9.0 / 7.0
    theta = 9.0 * bound / 16.0
    delta = 7.0 * bound / 16.0
    rho_0 = 1.0 / sigma
    rho_1 = 1.0 / (2.0 * sigma - rho_0)
    rho_2 = 1.0 / (2.0 * sigma - rho_1)

    def hand_over(h):
        return pltpu.make_async_remote_copy(
            src_ref=leaving.at[h],
            dst_ref=arrived_hbm.at[h],
            send_sem=coarse_sem.at[0, h],
            recv_sem=coarse_sem.at[1, h],
            device_id=opposite,
            device_id_type=MESH,
        )

    def store_later(h):
        return pltpu.make_async_copy(
            later.at[h], later_hbm.at[:, :, pl.ds(pl.multiple_of(h * half, half), half)], store_sem.at[0, h]
        )

    def store_kept(h):
        return pltpu.make_async_copy(
            kept.at[h], kept_hbm.at[:, pl.ds(pl.multiple_of(h * half, half), half)], store_sem.at[1, h]
        )

    def restricted(h, pair):
        total = None
        for i in range(2):
            x = 2 * pair + i
            term = jnp.dot(restrict[kind_ref[x]], residual[h, x].astype(BF16), preferred_element_type=F32)
            total = term if total is None else total + term
        return total

    def finish(r, h):
        @pl.when(r < ROUNDS - 1)
        def _():
            first = r == 0
            scale = jnp.where(first, rho_1 * rho_0, rho_2 * rho_1)
            gain = jnp.where(first, 2.0 * rho_1 / delta, 2.0 * rho_2 / delta)
            keep = jnp.where(first, 0.0, 1.0)

            def next_direction(x, carry):
                before = direction[h, x]
                value = scale * before + gain * residual[h, x]
                direction[h, x] = value
                later[h, x] = value + keep * before
                halo[r + 1, h, OWN, SELF, x] = value.astype(BF16)
                return carry

            lax.fori_loop(0, xb, next_direction, 0)
            send_own(r + 1, h)

        @pl.when(r == ROUNDS - 2)
        def _():
            store_later(h).start()

        @pl.when(r == ROUNDS - 1)
        def _():
            leaving[h] = restricted(h, 1 - parity).astype(BF16)
            hand_over(h).start()
            kept[h] = restricted(h, parity)
            store_kept(h).start()

    def half_step(t, older=True, newer=True):
        if older:
            r, h = lax.div(t - 1, HALVES), lax.rem(t - 1, HALVES)
        if newer:
            rn, hn = lax.div(t, HALVES), lax.rem(t, HALVES)

        def pass_near(piece):
            await_piece(rn, hn, NEAR, SELF, piece)
            near_to_ahead(rn, hn, piece).start()
            near_to_sib(rn, hn, piece).start()

        def pass_far(piece):
            await_piece(r, h, FAR, SELF, piece)
            far_to_sib(r, h, piece).start()

        if older:

            @pl.when(inner)
            def _():
                for piece in range(PIECES):
                    await_piece(r, h, NEAR, CROSS, piece)
                    cross_to_ahead(r, h, piece).start()

            await_row(r, h, OWN, SIB)
            apply(r, h, OWN, SIB)
            apply(r, h, NEAR, SELF)
            pass_far(0)
            await_row(r, h, NEAR, SIB)
            apply(r, h, NEAR, SIB)

            @pl.when(inner)
            def _():
                await_row(r, h, OWN, CROSS)
                apply(r, h, OWN, CROSS)
                apply(r, h, NEAR, CROSS)

            pass_far(1)
        if newer:
            pass_near(0)
        if older:

            @pl.when(has_far)
            def _():
                apply(r, h, FAR, SELF)

        if newer:
            pass_near(1)
        if older:
            await_row(r, h, FAR, SIB)

            @pl.when(has_far)
            def _():
                apply(r, h, FAR, SIB)

            @pl.when(inner)
            def _():
                await_row(r, h, FAR, CROSS)

            @pl.when(inner & has_far)
            def _():
                apply(r, h, FAR, CROSS)

            finish(r, h)
        if newer:
            apply(rn, hn, OWN, SELF)

    barrier = pltpu.get_barrier_semaphore()
    for device in (sibling, across, diagonal, opposite, ahead, behind):
        pl.semaphore_signal(barrier, inc=1, device_id=device, device_id_type=MESH)

    for h in range(HALVES):
        load_rhs[h].wait()

        def first_direction(x, carry):
            value = residual[h, x] / theta
            direction[h, x] = value
            halo[0, h, OWN, SELF, x] = value.astype(BF16)
            return carry

        lax.fori_loop(0, xb, first_direction, 0)
        if h == 0:
            pl.semaphore_wait(barrier, 6)
        send_own(0, h)
    for load in load_operator + [load_restrict]:
        load.wait()

    steps = ROUNDS * HALVES
    half_step(0, older=False)

    def middle(t, carry):
        half_step(t)
        return carry

    lax.fori_loop(1, steps, middle, 0)
    half_step(steps, newer=False)

    def drain(r, carry):
        for h in range(HALVES):
            for piece in range(PIECES):
                own_to_sib(r, h, piece).wait_send()
                own_to_opposite(r, h, piece).wait_send()
                near_to_sib(r, h, piece).wait_send()
                near_to_ahead(r, h, piece).wait_send()
                far_to_sib(r, h, piece).wait_send()

        @pl.when(inner)
        def _():
            for h in range(HALVES):
                for piece in range(PIECES):
                    own_to_across(r, h, piece).wait_send()
                    own_to_diagonal(r, h, piece).wait_send()
                    cross_to_ahead(r, h, piece).wait_send()

        return carry

    lax.fori_loop(0, ROUNDS, drain, 0)
    for h in range(HALVES):
        store_later(h).wait()
        store_kept(h).wait()
        hand_over(h).wait()


def on_device(layers, rhs, blocks, diag_blocks, neighbours, bound, restrict_blocks, restrict_kind):
    xb, width, cols = rhs.shape[2:]
    slots = blocks.shape[3]
    codes = neighbours[0, 0]
    codes = codes + (codes >= slots // 2).astype(jnp.int32)
    names = jnp.arange(slots + 1, dtype=jnp.int32)
    order = jnp.arange(slots, dtype=jnp.int32)
    slot_of = jnp.sum(jnp.where(codes[:, :, None] == names, order[:, None] - slots, 0), axis=1) + slots
    half = cols // HALVES
    smem = pl.BlockSpec(memory_space=pltpu.SMEM)
    hbm = pl.BlockSpec(memory_space=pl.ANY)
    later, kept, arrived = pl.pallas_call(
        functools.partial(smooth_kernel, layers),
        out_shape=(
            jax.ShapeDtypeStruct((xb, width, cols), F32),
            jax.ShapeDtypeStruct((width, cols), F32),
            jax.ShapeDtypeStruct((HALVES, width, half), BF16),
        ),
        in_specs=[smem, smem, smem, hbm, hbm, hbm, hbm],
        out_specs=(hbm, hbm, hbm),
        scratch_shapes=[
            pltpu.VMEM((xb, slots + 1, width, width), BF16),
            pltpu.VMEM((ROUNDS, HALVES, 3, 3, xb, width, half), BF16),
            pltpu.VMEM((HALVES, xb, width, half), F32),
            pltpu.VMEM((HALVES, xb, width, half), F32),
            pltpu.VMEM((HALVES, xb, width, half), F32),
            pltpu.VMEM(restrict_blocks.shape, BF16),
            pltpu.VMEM((HALVES, width, half), F32),
            pltpu.VMEM((HALVES, width, half), BF16),
            pltpu.SemaphoreType.DMA((4 + xb,)),
            pltpu.SemaphoreType.DMA((2, HALVES)),
            pltpu.SemaphoreType.DMA((ROUNDS, HALVES, 8, PIECES)),
            pltpu.SemaphoreType.DMA((ROUNDS, HALVES, 9, PIECES)),
            pltpu.SemaphoreType.DMA((2, HALVES)),
        ],
        compiler_params=pltpu.CompilerParams(
            collective_id=0, has_side_effects=True, vmem_limit_bytes=56 * 2**20
        ),
        cost_estimate=pl.CostEstimate(flops=6 * 10**9, bytes_accessed=11 * 10**6, transcendentals=0),
        name="smooth_and_restrict",
    )(slot_of, restrict_kind[0, 0], bound, rhs[0, 0], blocks[0, 0], diag_blocks[0, 0], restrict_blocks)
    smoothed = later + rhs[0, 0] / (9.0 * bound[0] / 16.0)
    coarse = kept + jnp.concatenate([arrived[h] for h in range(HALVES)], axis=1).astype(F32)
    return smoothed[None, None], coarse[None, None, None]


def solution(mesh):
    return jax.shard_map(
        functools.partial(on_device, mesh.shape["slab"]),
        mesh=mesh,
        in_specs=(
            P("slab", "quad", None, None, None),
            P("slab", "quad", None, None, None, None),
            P("slab", "quad", None, None, None),
            P("slab", "quad", None, None),
            P(),
            P(),
            P("slab", "quad", None),
        ),
        out_specs=(P("slab", "quad", None, None, None), P("slab", "quad", None, None, None)),
        check_vma=False,
    )
```

time: 209 us -> 74.4 us (0.36)
  the two profiles are of different devices: /device:TPU:125 before, /device:TPU:5 now
where the time goes in v2:
time: 74.4 us; the launch traced here: 73 us
  Pallas kernels  65.7 us (88%)
  other arithmetic  5.14 us (7%)
  between operations  1.29 us (2%)
  local copies, waits for them, and re-layouts  0.94 us (1%)
    pallas_call x1, Pallas kernels, on_device(): pl.pallas_call(functools.partial(smooth_kernel, layers), out_shape=(jax.S...  65.7 us
    broadcast_in_dim x2, other arithmetic, on_device(): return (smoothed[None, None], coarse[None, None, None])  3.74 us

profile of v2, /device:TPU:5, one launch (start us, length us, event | category | flops | bytes accessed | tf_op | source)
XLA Modules:
  0.0 73.0 jit_solution(2521610727186080095)
XLA Ops:
  1.3 0.7 bitcast_add_fusion
  2.0 0.1 copy.9
  2.1 0.1 select_reduce_fusion
  2.2 0.6 broadcast_add_fusion.slot_ref
  2.8 0.0 copy-start
  2.8 65.7 %smooth_and_restrict.1 = (f32[4,192,256]{2,1,0:T(8,128)}, f32[192,256]{1,0:T(8,128)}, bf16[2,192,128]{2,1,0:T(8,128)(2,1)}) custom-call(s32[4,27]{1,0:T(4,128)} %broadcast_add_fusion.slot_ref, s32[4]{0:T(128)} %bitcast.22, f32[1]{0:T(128)S(6)} %copy.10.bound_ref, f32[4,192,256]{2,1,0:T(8,128)} %bitcast.19, bf16[4,26,192,192]{3,2,1,0:T(8,128)(2,1)} %bitcast.20, ...), custom_call_target="tpu_custom_call" | custom-call | flops 6000000000 | bytes 11000000 | tf_op jit(solution)/shard_map/smooth_and_restrict/pallas_call | solution.py:345
  68.5 0.8 %slice_bitcast_fusion.1 = (bf16[192,128]{1,0:T(8,128)(2,1)S(1)}, bf16[192,128]{1,0:T(8,128)(2,1)S(1)}) fusion(bf16[2,192,128]{2,1,0:T(8,128)(2,1)} %get-tuple-element.7), kind=kLoop, calls=%fused_computation.5 | loop fusion | bytes 196608 | tf_op jit(solution)/shard_map/squeeze | solution.py:376
  69.3 1.6 %add_bitcast_fusion.1 = f32[1,1,1,192,256]{4,3,2,1,0:T(8,128)} fusion(f32[192,256]{1,0:T(8,128)} %get-tuple-element.6, bf16[192,128]{1,0:T(8,128)(2,1)S(1)} %get-tuple-element.9, bf16[192,128]{1,0:T(8,128)(2,1)S(1)} %get-tuple-element.8), kind=kLoop, calls=%fused_computation.1 | loop fusion | flops 245760 | bytes 491520 | tf_op jit(solution)/shard_map/broadcast_in_dim | solution.py:377
  70.9 0.0 copy-done
  70.9 2.1 %add_bitcast_fusion = f32[1,1,4,192,256]{4,3,2,1,0:T(8,128)} fusion(f32[4,192,256]{2,1,0:T(8,128)} %get-tuple-element.5, f32[]{:T(128)} %bitcast.5, f32[1,1,4,192,256]{4,3,2,1,0:T(8,128)S(1)} %copy-done), kind=kLoop, calls=%fused_computation | loop fusion | flops 393216 | bytes 2359300 | tf_op jit(solution)/shard_map/broadcast_in_dim | solution.py:377
  (1 shorter events, 0.0 us)
Async XLA Ops:
  2.8 68.1 %copy-start = (f32[1,1,4,192,256]{4,3,2,1,0:T(8,128)S(1)}, f32[1,1,4,192,256]{4,3,2,1,0:T(8,128)}, u32[]{:S(2)}) copy-start(f32[1,1,4,192,256]{4,3,2,1,0:T(8,128)} %param.7) | copy-start | bytes 2359300

commit v3 on v2

v3 whole, which is shorter than its diff:
```python
import functools

import jax
import jax.numpy as jnp
from jax import lax
from jax.experimental import pallas as pl
from jax.experimental.pallas import tpu as pltpu
from jax.sharding import PartitionSpec as P

OWN, NEAR, FAR = 0, 1, 2
SELF, SIB, CROSS = 0, 1, 2
ROUNDS = 3
HALVES = 2
PAIRS = (0, 2)
MESH = pl.DeviceIdType.MESH
F32 = jnp.float32
BF16 = jnp.bfloat16


def smooth_kernel(
    layers,
    kind_ref,
    bound_ref,
    code_hbm,
    rhs_hbm,
    blocks_hbm,
    diag_hbm,
    restrict_hbm,
    smoothed_hbm,
    kept_hbm,
    arrived_hbm,
    oper,
    halo,
    residual,
    direction,
    smoothed,
    restrict,
    kept,
    leaving,
    codes,
    columns,
    slot_ref,
    load_sem,
    store_sem,
    send_sem,
    recv_sem,
    coarse_sem,
):
    s = lax.axis_index("slab")
    q = lax.axis_index("quad")
    parity = lax.rem(s, 2)
    inner = (q == 1) | (q == 2)
    near_s = s + 1 - 2 * parity
    step = 2 - 4 * parity
    sibling = (s, q + 1 - 2 * lax.rem(q, 2))
    across = (s, 3 - q)
    diagonal = (near_s, 3 - q)
    opposite = (near_s, q)
    ahead = (lax.rem(s + step + layers, layers), q)
    behind = (lax.rem(s - step + layers, layers), q)
    dz_near = 2 - 2 * parity
    dy_sib = 2 - 2 * lax.rem(q, 2)
    has_far = jnp.where(parity == 0, s > 0, s < layers - 1)
    xb, width, half = residual.shape[1:]
    slots = blocks_hbm.shape[1]

    load_rhs = [
        pltpu.make_async_copy(rhs_hbm.at[:, :, pl.ds(h * half, half)], residual.at[h], load_sem.at[h])
        for h in range(HALVES)
    ]
    load_operator = [pltpu.make_async_copy(diag_hbm, oper.at[:, slots], load_sem.at[2])] + [
        pltpu.make_async_copy(blocks_hbm.at[x], oper.at[x, pl.ds(0, slots)], load_sem.at[3 + x]) for x in range(xb)
    ]
    load_restrict = pltpu.make_async_copy(restrict_hbm, restrict, load_sem.at[3 + xb])
    load_codes = pltpu.make_async_copy(code_hbm, codes, load_sem.at[4 + xb])
    place_slots = pltpu.make_async_copy(columns, slot_ref, load_sem.at[5 + xb])
    load_codes.start()
    for load in load_rhs + load_operator + [load_restrict]:
        load.start()

    def copy(r, h, lane, src, dst, device, first, count):
        blocks = pl.ds(first, count)
        return pltpu.make_async_remote_copy(
            src_ref=halo.at[r, h, src[0], src[1], blocks],
            dst_ref=halo.at[r, h, dst[0], dst[1], blocks],
            send_sem=send_sem.at[r, h, lane, first],
            recv_sem=recv_sem.at[r, h, dst[0] * 3 + dst[1], first],
            device_id=device,
            device_id_type=MESH,
        )

    def own_to_sib(r, h, first):
        return copy(r, h, 0, (OWN, SELF), (OWN, SIB), sibling, first, 2)

    def own_to_across(r, h, first):
        return copy(r, h, 1, (OWN, SELF), (OWN, CROSS), across, first, 2)

    def own_to_diagonal(r, h, first):
        return copy(r, h, 2, (OWN, SELF), (NEAR, CROSS), diagonal, first, 2)

    def own_to_opposite(r, h, first):
        return copy(r, h, 3, (OWN, SELF), (NEAR, SELF), opposite, first, 1)

    def near_to_sib(r, h, first):
        return copy(r, h, 4, (NEAR, SELF), (NEAR, SIB), sibling, first, 2)

    def near_to_ahead(r, h, first):
        return copy(r, h, 5, (NEAR, SELF), (FAR, SELF), ahead, first, 1)

    def cross_to_ahead(r, h, first):
        return copy(r, h, 6, (NEAR, CROSS), (FAR, CROSS), ahead, first, 2)

    def far_to_sib(r, h, first):
        return copy(r, h, 7, (FAR, SELF), (FAR, SIB), sibling, first, 1)

    def await_piece(r, h, a, b, first, count):
        copy(r, h, 0, (a, b), (a, b), sibling, first, count).wait_recv()

    def await_pairs(r, h, a, b):
        for first in PAIRS:
            await_piece(r, h, a, b, first, 2)

    def send_pair(r, h, first):
        @pl.when(inner)
        def _():
            own_to_diagonal(r, h, first).start()

        own_to_sib(r, h, first).start()

        @pl.when(inner)
        def _():
            own_to_across(r, h, first).start()

    def apply(r, h, a, b, sources=range(4)):
        dz = (1, dz_near, 2 - dz_near)[a]
        dy = (1, dy_sib, 2 - dy_sib)[b]
        base = dz * 9 + dy * 3
        for source in sources:
            targets = [x for x in (source - 1, source, source + 1) if 0 <= x < xb]
            rows = [oper[x, slot_ref[base + source - x + 1, x]] for x in targets]
            moved = jnp.dot(jnp.concatenate(rows, axis=0), halo[r, h, a, b, source], preferred_element_type=F32)
            for i, x in enumerate(targets):
                residual[h, x] -= moved[i * width : (i + 1) * width]

    bound = bound_ref[0]
    sigma = 9.0 / 7.0
    theta = 9.0 * bound / 16.0
    delta = 7.0 * bound / 16.0
    rho_0 = 1.0 / sigma
    rho_1 = 1.0 / (2.0 * sigma - rho_0)
    rho_2 = 1.0 / (2.0 * sigma - rho_1)

    def hand_over(h):
        return pltpu.make_async_remote_copy(
            src_ref=leaving.at[h],
            dst_ref=arrived_hbm.at[h],
            send_sem=coarse_sem.at[0, h],
            recv_sem=coarse_sem.at[1, h],
            device_id=opposite,
            device_id_type=MESH,
        )

    def store_smoothed(h):
        return pltpu.make_async_copy(
            smoothed.at[h], smoothed_hbm.at[:, :, pl.ds(pl.multiple_of(h * half, half), half)], store_sem.at[0, h]
        )

    def store_kept(h):
        return pltpu.make_async_copy(
            kept.at[h], kept_hbm.at[:, pl.ds(pl.multiple_of(h * half, half), half)], store_sem.at[1, h]
        )

    def restricted(h, pair):
        total = None
        for i in range(2):
            x = 2 * pair + i
            term = jnp.dot(restrict[kind_ref[x]], residual[h, x].astype(BF16), preferred_element_type=F32)
            total = term if total is None else total + term
        return total

    def advance(r, h, targets):
        @pl.when(r < ROUNDS - 1)
        def _():
            first = r == 0
            scale = jnp.where(first, rho_1 * rho_0, rho_2 * rho_1)
            gain = jnp.where(first, 2.0 * rho_1 / delta, 2.0 * rho_2 / delta)
            for x in targets:
                value = scale * direction[h, x] + gain * residual[h, x]
                direction[h, x] = value
                smoothed[h, x] += value
                halo[r + 1, h, OWN, SELF, x] = value.astype(BF16)
                own_to_opposite(r + 1, h, x).start()
                if x % 2 == 1:
                    send_pair(r + 1, h, x - 1)

    def finish(r, h):
        @pl.when(r == ROUNDS - 2)
        def _():
            store_smoothed(h).start()

        @pl.when(r == ROUNDS - 1)
        def _():
            leaving[h] = restricted(h, 1 - parity).astype(BF16)
            hand_over(h).start()
            kept[h] = restricted(h, parity)
            store_kept(h).start()

    def half_step(t, last=True, older=True, newer=True):
        if last:
            rl, hl = lax.div(t - 2, HALVES), lax.rem(t, HALVES)
        if older:
            r, h = lax.div(t - 1, HALVES), lax.rem(t - 1, HALVES)
        if newer:
            rn, hn = lax.div(t, HALVES), lax.rem(t, HALVES)

        def pass_near(r, h, x):
            await_piece(r, h, NEAR, SELF, x, 1)
            near_to_ahead(r, h, x).start()
            if x % 2 == 1:
                near_to_sib(r, h, x - 1).start()

        def pass_far(x):
            await_piece(r, h, FAR, SELF, x, 1)
            far_to_sib(r, h, x).start()

        def far_blocks(row, sources):
            @pl.when((inner & has_far) if row == CROSS else has_far)
            def _():
                apply(r, h, FAR, row, sources)

        if older:
            pass_near(r, h, 3)

            @pl.when(inner)
            def _():
                for first in PAIRS:
                    await_piece(r, h, NEAR, CROSS, first, 2)
                    cross_to_ahead(r, h, first).start()

            apply(r, h, OWN, SELF)
        if last:
            await_piece(rl, hl, FAR, SIB, 3, 1)

            @pl.when(has_far)
            def _():
                apply(rl, hl, FAR, SIB, (3,))

            advance(rl, hl, (2, 3))
            finish(rl, hl)
        if older:
            await_pairs(r, h, OWN, SIB)
            apply(r, h, OWN, SIB)
            pass_far(0)
            apply(r, h, NEAR, SELF)

            @pl.when(inner)
            def _():
                await_pairs(r, h, OWN, CROSS)
                apply(r, h, OWN, CROSS)

            pass_far(1)
        if newer:
            pass_near(rn, hn, 0)
        if older:
            await_pairs(r, h, NEAR, SIB)
            apply(r, h, NEAR, SIB)

            @pl.when(inner)
            def _():
                apply(r, h, NEAR, CROSS)

            far_blocks(SELF, (0, 1))
            pass_far(2)
            for x in (0, 1):
                await_piece(r, h, FAR, SIB, x, 1)
            far_blocks(SIB, (0, 1))

            @pl.when(inner)
            def _():
                await_piece(r, h, FAR, CROSS, 0, 2)

            far_blocks(CROSS, (0, 1))
            advance(r, h, (0,))
        if newer:
            pass_near(rn, hn, 1)
            pass_near(rn, hn, 2)
        if older:
            pass_far(3)
            far_blocks(SELF, (2, 3))

            @pl.when(inner)
            def _():
                await_piece(r, h, FAR, CROSS, 2, 2)

            far_blocks(CROSS, (2, 3))
            await_piece(r, h, FAR, SIB, 2, 1)
            far_blocks(SIB, (2,))
            advance(r, h, (1,))

    barrier = pltpu.get_barrier_semaphore()
    for device in (sibling, across, diagonal, opposite, ahead, behind):
        pl.semaphore_signal(barrier, inc=1, device_id=device, device_id_type=MESH)

    for h in range(HALVES):
        load_rhs[h].wait()

        def first_direction(x, carry):
            value = residual[h, x] / theta
            direction[h, x] = value
            smoothed[h, x] = value
            halo[0, h, OWN, SELF, x] = value.astype(BF16)
            return carry

        lax.fori_loop(0, xb, first_direction, 0)
        if h == 0:
            pl.semaphore_wait(barrier, 6)
        for x in range(xb):
            own_to_opposite(0, h, x).start()
        for first in PAIRS:
            send_pair(0, h, first)

    load_codes.wait()
    shape = (columns.shape[0], slots)
    offset = lax.broadcasted_iota(jnp.int32, shape, 0)
    slot = lax.broadcasted_iota(jnp.int32, shape, 1)
    lane = lax.broadcasted_iota(jnp.int32, columns.shape, 1)
    table = jnp.zeros(columns.shape, jnp.int32)
    for x in range(xb):
        named = codes[pl.ds(x, 1), :]
        named = named + jnp.where(named >= slots // 2, 1, 0)
        found = jnp.min(jnp.where(named == offset, slot, slots), axis=1, keepdims=True)
        table = jnp.where(lane == x, found, table)
    columns[...] = table
    place_slots.start()
    for load in load_operator + [load_restrict, place_slots]:
        load.wait()

    steps = ROUNDS * HALVES
    half_step(0, last=False, older=False)
    half_step(1, last=False)

    def middle(t, carry):
        half_step(t)
        return carry

    lax.fori_loop(2, steps, middle, 0)
    half_step(steps, newer=False)
    half_step(steps + 1, older=False, newer=False)

    def drain(r, carry):
        for h in range(HALVES):
            for x in range(xb):
                own_to_opposite(r, h, x).wait_send()
                near_to_ahead(r, h, x).wait_send()
                far_to_sib(r, h, x).wait_send()
            for first in PAIRS:
                own_to_sib(r, h, first).wait_send()
                near_to_sib(r, h, first).wait_send()

        @pl.when(inner)
        def _():
            for h in range(HALVES):
                for first in PAIRS:
                    own_to_across(r, h, first).wait_send()
                    own_to_diagonal(r, h, first).wait_send()
                    cross_to_ahead(r, h, first).wait_send()

        return carry

    lax.fori_loop(0, ROUNDS, drain, 0)
    for h in range(HALVES):
        store_smoothed(h).wait()
        store_kept(h).wait()
        hand_over(h).wait()


def outputs_kernel(smoothed_in, kept_in, arrived_in, smoothed_out, coarse_out, smoothed, coarse, arrived, sem):
    load_arrived = pltpu.make_async_copy(arrived_in, arrived, sem.at[0])
    load_kept = pltpu.make_async_copy(kept_in, coarse, sem.at[1])
    store = pltpu.make_async_copy(coarse, coarse_out, sem.at[2])
    load_arrived.start()
    load_kept.start()
    blocks = range(smoothed.shape[0])
    loads = [pltpu.make_async_copy(smoothed_in.at[x], smoothed.at[x], sem.at[3 + 2 * x]) for x in blocks]
    stores = [pltpu.make_async_copy(smoothed.at[x], smoothed_out.at[x], sem.at[4 + 2 * x]) for x in blocks]
    for load in loads:
        load.start()
    load_arrived.wait()
    load_kept.wait()
    coarse[...] += jnp.concatenate([arrived[h] for h in range(HALVES)], axis=1).astype(F32)
    store.start()
    for x in blocks:
        loads[x].wait()
        stores[x].start()
    for x in blocks:
        stores[x].wait()
    store.wait()


def on_device(layers, rhs, blocks, diag_blocks, neighbours, bound, restrict_blocks, restrict_kind):
    xb, width, cols = rhs.shape[2:]
    slots = blocks.shape[3]
    half = cols // HALVES
    smem = pl.BlockSpec(memory_space=pltpu.SMEM)
    hbm = pl.BlockSpec(memory_space=pl.ANY)
    smoothed, kept, arrived = pl.pallas_call(
        functools.partial(smooth_kernel, layers),
        out_shape=(
            jax.ShapeDtypeStruct((xb, width, cols), F32),
            jax.ShapeDtypeStruct((width, cols), F32),
            jax.ShapeDtypeStruct((HALVES, width, half), BF16),
        ),
        in_specs=[smem, smem, hbm, hbm, hbm, hbm, hbm],
        out_specs=(hbm, hbm, hbm),
        scratch_shapes=[
            pltpu.VMEM((xb, slots + 1, width, width), BF16),
            pltpu.VMEM((ROUNDS, HALVES, 3, 3, xb, width, half), BF16),
            pltpu.VMEM((HALVES, xb, width, half), F32),
            pltpu.VMEM((HALVES, xb, width, half), F32),
            pltpu.VMEM((HALVES, xb, width, half), F32),
            pltpu.VMEM(restrict_blocks.shape, BF16),
            pltpu.VMEM((HALVES, width, half), F32),
            pltpu.VMEM((HALVES, width, half), BF16),
            pltpu.VMEM((xb, slots), jnp.int32),
            pltpu.VMEM((32, 128), jnp.int32),
            pltpu.SMEM((32, 128), jnp.int32),
            pltpu.SemaphoreType.DMA((6 + xb,)),
            pltpu.SemaphoreType.DMA((2, HALVES)),
            pltpu.SemaphoreType.DMA((ROUNDS, HALVES, 8, xb)),
            pltpu.SemaphoreType.DMA((ROUNDS, HALVES, 9, xb)),
            pltpu.SemaphoreType.DMA((2, HALVES)),
        ],
        compiler_params=pltpu.CompilerParams(
            collective_id=0, has_side_effects=True, vmem_limit_bytes=56 * 2**20
        ),
        cost_estimate=pl.CostEstimate(flops=6 * 10**9, bytes_accessed=11 * 10**6, transcendentals=0),
        name="smooth_and_restrict",
    )(restrict_kind[0, 0], bound, neighbours[0, 0], rhs[0, 0], blocks[0, 0], diag_blocks[0, 0], restrict_blocks)
    smoothed, coarse = pl.pallas_call(
        outputs_kernel,
        out_shape=(
            jax.ShapeDtypeStruct((xb, width, cols), F32),
            jax.ShapeDtypeStruct((width, cols), F32),
        ),
        in_specs=[hbm, hbm, hbm],
        out_specs=(hbm, hbm),
        scratch_shapes=[
            pltpu.VMEM((xb, width, cols), F32),
            pltpu.VMEM((width, cols), F32),
            pltpu.VMEM((HALVES, width, half), BF16),
            pltpu.SemaphoreType.DMA((3 + 2 * xb,)),
        ],
        compiler_params=pltpu.CompilerParams(vmem_limit_bytes=56 * 2**20),
        name="outputs",
    )(smoothed, kept, arrived)
    return smoothed[None, None], coarse[None, None, None]


def solution(mesh):
    return jax.shard_map(
        functools.partial(on_device, mesh.shape["slab"]),
        mesh=mesh,
        in_specs=(
            P("slab", "quad", None, None, None),
            P("slab", "quad", None, None, None, None),
            P("slab", "quad", None, None, None),
            P("slab", "quad", None, None),
            P(),
            P(),
            P("slab", "quad", None),
        ),
        out_specs=(P("slab", "quad", None, None, None), P("slab", "quad", None, None, None)),
        check_vma=False,
    )
```

time: 74.4 us -> 71 us (0.954); the launches traced: 73 us -> 70.8 us
  other arithmetic: 5.14 us -> 0 us
  Pallas kernels: 65.7 us -> 69.5 us
  local copies, waits for them, and re-layouts: 0.94 us -> 0 us
    broadcast_in_dim x2 -> x0, other arithmetic: 3.74 us -> none  [on_device(): return (smoothed[None, None], coarse[None, None, None])]
    pallas_call x0 -> x1, Pallas kernels: none -> 2.1 us  [on_device(): pl.pallas_call(outputs_kernel, out_shape=(jax.ShapeDtypeStruct((xb, width...]
    pallas_call x1, Pallas kernels: 65.7 us -> 67.4 us  [on_device(): pl.pallas_call(functools.partial(smooth_kernel, layers), out_shape=(jax.S...]
    add x2 -> x0, other arithmetic: 1.27 us -> none  [the longest x1 0.69 us: on_device(): codes = codes + (codes >= slots // 2).astype(jnp.int32)]
    squeeze x1 -> x0, local copies, waits for them, and re-layouts: 0.83 us -> none  [on_device(): arrived[h]]
where the time goes in v3:
time: 71 us; the launch traced here: 70.8 us
  Pallas kernels  69.5 us (98%)
  between operations  1.29 us (2%)
    pallas_call x1, Pallas kernels, on_device(): pl.pallas_call(functools.partial(smooth_kernel, layers), out_shape=(jax.S...  67.4 us
    pallas_call x1, Pallas kernels, on_device(): pl.pallas_call(outputs_kernel, out_shape=(jax.ShapeDtypeStruct((xb, width...  2.1 us

profile of v3, /device:TPU:5, one launch (start us, length us, event | category | flops | bytes accessed | tf_op | source)
XLA Modules:
  0.0 70.8 jit_solution(6871010289748488815)
XLA Ops:
  1.3 67.4 %smooth_and_restrict.1 = (f32[4,192,256]{2,1,0:T(8,128)}, f32[192,256]{1,0:T(8,128)}, bf16[2,192,128]{2,1,0:T(8,128)(2,1)}) custom-call(s32[4]{0:T(128)} %bitcast.13, f32[1]{0:T(128)S(6)} %copy.9.bound_ref, s32[4,26]{1,0:T(4,128)} %bitcast.12, f32[4,192,256]{2,1,0:T(8,128)} %bitcast.8, bf16[4,26,192,192]{3,2,1,0:T(8,128)(2,1)} %bitcast.7, ...), custom_call_target="tpu_custom_call" | custom-call | flops 6000000000 | bytes 11000000 | tf_op jit(solution)/shard_map/smooth_and_restrict/pallas_call | solution.py:406
  68.7 2.1 %outputs.1 = (f32[4,192,256]{2,1,0:T(8,128)}, f32[192,256]{1,0:T(8,128)}) custom-call(f32[4,192,256]{2,1,0:T(8,128)} %get-tuple-element.7.smoothed_in, f32[192,256]{1,0:T(8,128)} %get-tuple-element.8.kept_in, bf16[2,192,128]{2,1,0:T(8,128)(2,1)} %get-tuple-element.9.arrived_in), custom_call_target="tpu_custom_call" | custom-call | tf_op jit(solution)/shard_map/outputs/pallas_call | solution.py:439

commit v4 on v3

--- a/solution.py
+++ b/solution.py
@@ -75,7 +75,7 @@
     load_codes = pltpu.make_async_copy(code_hbm, codes, load_sem.at[4 + xb])
     place_slots = pltpu.make_async_copy(columns, slot_ref, load_sem.at[5 + xb])
     load_codes.start()
-    for load in load_rhs + load_operator + [load_restrict]:
+    for load in load_rhs:
         load.start()
 
     def copy(r, h, lane, src, dst, device, first, count):
@@ -281,11 +281,12 @@
 
             far_blocks(CROSS, (0, 1))
             advance(r, h, (0,))
+        if older:
+            pass_far(3)
         if newer:
             pass_near(rn, hn, 1)
             pass_near(rn, hn, 2)
         if older:
-            pass_far(3)
             far_blocks(SELF, (2, 3))
 
             @pl.when(inner)
@@ -312,6 +313,9 @@
             return carry
 
         lax.fori_loop(0, xb, first_direction, 0)
+        if h == HALVES - 1:
+            for load in load_operator + [load_restrict]:
+                load.start()
         if h == 0:
             pl.semaphore_wait(barrier, 6)
         for x in range(xb):
@@ -332,11 +336,11 @@
         table = jnp.where(lane == x, found, table)
     columns[...] = table
     place_slots.start()
+
+    steps = ROUNDS * HALVES
+    half_step(0, last=False, older=False)
     for load in load_operator + [load_restrict, place_slots]:
         load.wait()
-
-    steps = ROUNDS * HALVES
-    half_step(0, last=False, older=False)
     half_step(1, last=False)
 
     def middle(t, carry):

time: 71 us -> 71.3 us (level)
  no operation moved by 1% of the time
where the time goes in v4:
time: 71.3 us; the launch traced here: 70.8 us
  Pallas kernels  69.5 us (97%)
  between operations  1.29 us (2%)
    pallas_call x1, Pallas kernels, on_device(): pl.pallas_call(functools.partial(smooth_kernel, layers), out_shape=(jax.S...  67.4 us
    pallas_call x1, Pallas kernels, on_device(): pl.pallas_call(outputs_kernel, out_shape=(jax.ShapeDtypeStruct((xb, width...  2.1 us

profile of v4, /device:TPU:5, one launch (start us, length us, event | category | flops | bytes accessed | tf_op | source)
XLA Modules:
  0.0 70.8 jit_solution(14449283281130445786)
XLA Ops:
  1.3 67.4 %smooth_and_restrict.1 = (f32[4,192,256]{2,1,0:T(8,128)}, f32[192,256]{1,0:T(8,128)}, bf16[2,192,128]{2,1,0:T(8,128)(2,1)}) custom-call(s32[4]{0:T(128)} %bitcast.13, f32[1]{0:T(128)S(6)} %copy.9.bound_ref, s32[4,26]{1,0:T(4,128)} %bitcast.12, f32[4,192,256]{2,1,0:T(8,128)} %bitcast.8, bf16[4,26,192,192]{3,2,1,0:T(8,128)(2,1)} %bitcast.7, ...), custom_call_target="tpu_custom_call" | custom-call | flops 6000000000 | bytes 11000000 | tf_op jit(solution)/shard_map/smooth_and_restrict/pallas_call | solution.py:410
  68.7 2.1 %outputs.1 = (f32[4,192,256]{2,1,0:T(8,128)}, f32[192,256]{1,0:T(8,128)}) custom-call(f32[4,192,256]{2,1,0:T(8,128)} %get-tuple-element.7.smoothed_in, f32[192,256]{1,0:T(8,128)} %get-tuple-element.8.kept_in, bf16[2,192,128]{2,1,0:T(8,128)(2,1)} %get-tuple-element.9.arrived_in), custom_call_target="tpu_custom_call" | custom-call | tf_op jit(solution)/shard_map/outputs/pallas_call | solution.py:443

commit v5 on v4

--- a/solution.py
+++ b/solution.py
@@ -237,7 +237,6 @@
                     await_piece(r, h, NEAR, CROSS, first, 2)
                     cross_to_ahead(r, h, first).start()
 
-            apply(r, h, OWN, SELF)
         if last:
             await_piece(rl, hl, FAR, SIB, 3, 1)
 
@@ -248,6 +247,7 @@
             advance(rl, hl, (2, 3))
             finish(rl, hl)
         if older:
+            apply(r, h, OWN, SELF)
             await_pairs(r, h, OWN, SIB)
             apply(r, h, OWN, SIB)
             pass_far(0)
@@ -287,16 +287,18 @@
             pass_near(rn, hn, 1)
             pass_near(rn, hn, 2)
         if older:
-            far_blocks(SELF, (2, 3))
+            far_blocks(SELF, (2,))
 
             @pl.when(inner)
             def _():
                 await_piece(r, h, FAR, CROSS, 2, 2)
 
-            far_blocks(CROSS, (2, 3))
+            far_blocks(CROSS, (2,))
             await_piece(r, h, FAR, SIB, 2, 1)
             far_blocks(SIB, (2,))
             advance(r, h, (1,))
+            far_blocks(SELF, (3,))
+            far_blocks(CROSS, (3,))
 
     barrier = pltpu.get_barrier_semaphore()
     for device in (sibling, across, diagonal, opposite, ahead, behind):

time: 71.3 us -> 70.9 us (level)
  no operation moved by 1% of the time
where the time goes in v5:
time: 70.9 us; the launch traced here: 70.8 us
  Pallas kernels  69.5 us (98%)
  between operations  1.29 us (2%)
    pallas_call x1, Pallas kernels, on_device(): pl.pallas_call(functools.partial(smooth_kernel, layers), out_shape=(jax.S...  67.4 us
    pallas_call x1, Pallas kernels, on_device(): pl.pallas_call(outputs_kernel, out_shape=(jax.ShapeDtypeStruct((xb, width...  2.1 us

profile of v5, /device:TPU:5, one launch (start us, length us, event | category | flops | bytes accessed | tf_op | source)
XLA Modules:
  0.0 70.8 jit_solution(16316641267169251944)
XLA Ops:
  1.3 67.4 %smooth_and_restrict.1 = (f32[4,192,256]{2,1,0:T(8,128)}, f32[192,256]{1,0:T(8,128)}, bf16[2,192,128]{2,1,0:T(8,128)(2,1)}) custom-call(s32[4]{0:T(128)} %bitcast.13, f32[1]{0:T(128)S(6)} %copy.9.bound_ref, s32[4,26]{1,0:T(4,128)} %bitcast.12, f32[4,192,256]{2,1,0:T(8,128)} %bitcast.8, bf16[4,26,192,192]{3,2,1,0:T(8,128)(2,1)} %bitcast.7, ...), custom_call_target="tpu_custom_call" | custom-call | flops 6000000000 | bytes 11000000 | tf_op jit(solution)/shard_map/smooth_and_restrict/pallas_call | solution.py:412
  68.7 2.1 %outputs.1 = (f32[4,192,256]{2,1,0:T(8,128)}, f32[192,256]{1,0:T(8,128)}) custom-call(f32[4,192,256]{2,1,0:T(8,128)} %get-tuple-element.7.smoothed_in, f32[192,256]{1,0:T(8,128)} %get-tuple-element.8.kept_in, bf16[2,192,128]{2,1,0:T(8,128)(2,1)} %get-tuple-element.9.arrived_in), custom_call_target="tpu_custom_call" | custom-call | tf_op jit(solution)/shard_map/outputs/pallas_call | solution.py:445
